TPU v7x, 1024 devices: a whole 4x8x16 slice. The times are simulated.
1024 devices in a mesh: ctx: 16 (over z), exp: 64 (over y, x, core).
Axes of the slice: x: 4, y: 8, z: 16, core: 2. Of those that a mesh axis runs over, the one named last changes fastest.
Arguments:
- queries: bfloat16 [2048, 8192], P('ctx', 'exp'), may hold values from -30 to 30
- keyvals: bfloat16 [2, 2048, 512], P(None, 'ctx'), may hold values from -7 to 7
- d_attn: bfloat16 [2048, 8192], P('ctx', 'exp'), may hold values from -6 to 6
- grad_tokens: bfloat16 [8192, 4096], P(('ctx', 'exp')), may hold values from -6 to 6
- expert_ids: int32 [8192, 8], P(('ctx', 'exp')), may hold values from 0 to 63, all different within a row; in each aligned block of 8 rows (0 to 7, 8 to 15, ...) at most 2 rows name the same one
- route_weights: float32 [8192, 8], P(('ctx', 'exp')), may hold values from 0.05 to 0.3
- saved_gate_up: bfloat16 [16, 64, 128, 1536], P('ctx', 'exp'), may hold values from -6 to 6
- down_weight: bfloat16 [64, 768, 4096], P('exp'), may hold values from -0.21875 to 0.21875
Outputs:
- d_queries: bfloat16 [2048, 8192], P('ctx', 'exp')
- d_keyvals: float32 [2048, 4, 256], P(('ctx', 'exp'))
- d_gate_up: bfloat16 [16, 64, 128, 1536], P('ctx', 'exp')
Inputs may be any that keep to these rules, and one draw needn't show every extreme that they name: `expert_ids`: each row names 8 different experts; among the rows of one device no expert is named more than 2 times.
All inputs are finite; a program needn't handle non-finite values.
Results may differ from a plain program's by a relative error of at most 0.011.
Values may be sent and summed in bfloat16 or wider, within the bound.
A program may use at most 32 MiB of HBM per device.

v0:
```python
import math

import jax
import jax.numpy as jnp
from jax import lax
from jax.sharding import PartitionSpec as P

contract_first = (((0,), (0,)), ((), ()))
contract_last = (((1,), (1,)), ((), ()))


def body(
    queries, keyvals, d_attn, grad_tokens, expert_ids, route_weights, saved_gate_up, down_weight
):
    row_count = queries.shape[0]
    head_dim = queries.shape[1]
    kv_count = keyvals.shape[2] // head_dim
    exp_count = lax.axis_size("exp")
    group_width = exp_count // kv_count
    kv_group = lax.axis_index("exp") // group_width
    score_scale = 1.0 / math.sqrt(head_dim)
    own_pair = lax.dynamic_slice_in_dim(keyvals, kv_group * head_dim, head_dim, 2)
    all_pairs = lax.all_gather(own_pair, "ctx", axis=1, tiled=True)
    every_key = all_pairs[0]
    every_value = all_pairs[1]
    length = every_key.shape[0]
    offset = lax.axis_index("ctx") * row_count
    query_positions = offset + jnp.arange(row_count)
    causal = jnp.arange(length)[None, :] <= query_positions[:, None]
    scores = (
        lax.dot_general(queries, every_key, contract_last, preferred_element_type=jnp.float32)
        * score_scale
    )
    scores = jnp.where(causal, scores, -jnp.inf)
    highest = jnp.max(scores, axis=1, keepdims=True)
    log_total = highest[:, 0] + jnp.log(jnp.sum(jnp.exp(scores - highest), axis=1))
    softmax = jnp.exp(scores - log_total[:, None])
    softmax_b = softmax.astype(jnp.bfloat16)
    attended = jnp.dot(softmax_b, every_value, preferred_element_type=jnp.float32)
    row_delta = jnp.sum(d_attn.astype(jnp.float32) * attended, axis=1)
    d_softmax = lax.dot_general(
        d_attn, every_value, contract_last, preferred_element_type=jnp.float32
    )
    d_scores = (softmax * (d_softmax - row_delta[:, None])).astype(jnp.bfloat16)
    d_queries = (
        jnp.dot(d_scores, every_key, preferred_element_type=jnp.float32) * score_scale
    ).astype(jnp.bfloat16)
    key_grad = (
        lax.dot_general(d_scores, queries, contract_first, preferred_element_type=jnp.float32)
        * score_scale
    )
    value_grad = lax.dot_general(
        softmax_b, d_attn, contract_first, preferred_element_type=jnp.float32
    )
    key_grads = lax.psum_scatter(
        jnp.concatenate([key_grad, value_grad], axis=1), "ctx", scatter_dimension=0, tiled=True
    )
    from_heads = lax.all_to_all(
        key_grads.reshape(1, row_count, 2 * head_dim),
        "exp",
        split_axis=1,
        concat_axis=0,
        tiled=True,
    )
    grouped = jnp.sum(
        from_heads.reshape(kv_count, group_width, row_count // exp_count, 2 * head_dim), axis=1
    )
    d_keyvals = jnp.transpose(grouped, (1, 0, 2))
    token_count = grad_tokens.shape[0]
    choice_count = expert_ids.shape[1]
    width = grad_tokens.shape[1]
    hidden_width = down_weight.shape[1]
    capacity = saved_gate_up.shape[2] // exp_count
    chosen = (expert_ids[:, :, None] == jnp.arange(exp_count)[None, None, :]).astype(jnp.int32)
    per_row = jnp.sum(chosen, axis=1)
    before = jnp.cumsum(per_row, axis=0) - per_row
    slot_index = jnp.sum(chosen * before[:, None, :], axis=2)
    target = (expert_ids * capacity + slot_index).reshape(-1)
    placer = (target[None, :] == jnp.arange(exp_count * capacity)[:, None]).astype(jnp.bfloat16)
    scaled = (route_weights[:, :, None] * grad_tokens.astype(jnp.float32)[:, None, :]).astype(
        jnp.bfloat16
    )
    scaled = scaled.reshape(token_count * choice_count, width)
    outgoing = jnp.dot(placer, scaled, preferred_element_type=jnp.float32).astype(jnp.bfloat16)
    outgoing = outgoing.reshape(exp_count, capacity, width)
    incoming = lax.all_to_all(outgoing, "exp", split_axis=0, concat_axis=0, tiled=True)
    d_hidden = lax.dot_general(
        incoming.reshape(exp_count * capacity, width),
        down_weight[0],
        contract_last,
        preferred_element_type=jnp.float32,
    )
    stored = saved_gate_up[0, 0].astype(jnp.float32)
    gate_part = stored[:, :hidden_width]
    up_part = stored[:, hidden_width:]
    sigmoid_gate = 1.0 / (1.0 + jnp.exp(-gate_part))
    d_gate = d_hidden * up_part * sigmoid_gate * (1.0 + gate_part * (1.0 - sigmoid_gate))
    d_up = d_hidden * gate_part * sigmoid_gate
    d_gate_up = jnp.concatenate([d_gate, d_up], axis=1).astype(jnp.bfloat16)[None, None]
    return (d_queries, d_keyvals, d_gate_up)


def solution(mesh):
    placed = (
        P("ctx", "exp"),
        P(None, "ctx", None),
        P("ctx", "exp"),
        P(("ctx", "exp"), None),
        P(("ctx", "exp"), None),
        P(("ctx", "exp"), None),
        P("ctx", "exp", None, None),
        P("exp", None, None),
    )
    return jax.shard_map(
        body,
        mesh=mesh,
        in_specs=placed,
        out_specs=(P("ctx", "exp"), P(("ctx", "exp"), None, None), P("ctx", "exp", None, None)),
        check_vma=False,
    )
```

profile of v0, /device:TPU:1, one launch (start us, length us, event | category | flops | bytes accessed | tf_op | source)
XLA Modules:
  0.0 204.4 jit_solution(15115753371055860091)
XLA Ops:
  7.2 0.0 copy-start
  7.2 0.0 copy-start.4
  7.2 0.0 all-gather.2.cloned.1.call-start
  7.3 0.9 copy-done
  8.1 0.6 constant_dynamic-slice_fusion
  8.8 0.0 all-gather.2.cloned.1.call-update
  8.8 0.0 reduce-scatter.2.cloned.1.call-start
  8.8 0.9 copy.19
  9.7 75.5 %all-gather.2.cloned.1.call-done = bf16[2,2048,128]{2,1,0:T(8,128)(2,1)} async-done(((bf16[2,128,128]{2,1,0:T(8,128)(2,1)}), bf16[2,2048,128]{2,1,0:T(8,128)(2,1)}) %all-gather.2.cloned.1.call-update) | async-done | bytes 1048592 | tf_op jit(solution)/shard_map/all_gather | solution.py:23
  85.2 0.0 copy-start.1
  85.2 1.6 fusion.23
  86.8 0.3 exponential_reduce_fusion
  87.1 0.0 copy-done.4
  87.1 0.3 fusion.19
  87.4 0.0 copy-done.1
  87.4 0.0 copy-start.7
  87.5 0.4 fusion.8
  87.9 0.3 fusion.6
  88.2 0.0 copy-done.7
  88.3 0.3 convolution_multiply_fusion
  88.5 1.5 pad_maximum_fusion
  90.0 0.0 copy-start.5
  90.0 0.0 copy-start.8
  90.0 0.0 copy-start.6
  90.0 0.0 reduce-scatter.2.cloned.1.call-update
  90.1 0.8 copy-done.5
  90.9 0.0 copy-done.8
  90.9 0.1 mul.95
  91.0 0.0 copy-done.6
  91.0 0.1 convert_reduce_fusion
  91.1 0.3 select_reduce_fusion
  91.4 0.1 eq.31
  91.5 0.5 convolution_convert_fusion
  92.0 1.5 reshape.86
  93.5 0.0 copy-start.3
  93.5 20.0 %all-to-all-start.1 = ((bf16[64,2,4096]{2,1,0:T(2,128)(2,1)}), bf16[64,2,4096]{2,1,0:T(2,128)(2,1)S(1)}, u32[]{:S(2)}, u32[]{:S(2)}) async-start(bf16[64,2,4096]{2,1,0:T(2,128)(2,1)} %reshape.86), calls=%async_computation.2 | async-start | bytes 2097152 | tf_op jit(solution)/shard_map/all_to_all | solution.py:86
  113.5 0.0 copy-done.3
  113.5 1.0 bitcast_convert_fusion
  114.5 1.0 fusion.7
  115.4 0.0 copy-start.2
  115.4 26.1 %all-to-all-done.1 = bf16[64,2,4096]{2,1,0:T(2,128)(2,1)S(1)} async-done(((bf16[64,2,4096]{2,1,0:T(2,128)(2,1)}), bf16[64,2,4096]{2,1,0:T(2,128)(2,1)S(1)}, u32[]{:S(2)}, u32[]{:S(2)}) %all-to-all-start.1) | async-done | bytes 1048608 | tf_op jit(solution)/shard_map/all_to_all | solution.py:86
  141.5 0.4 reshape.87
  141.9 21.7 %reduce-scatter.2.cloned.1.call-done = f32[128,256]{1,0:T(8,128)} async-done(((f32[2048,256]{1,0:T(8,128)}), f32[128,256]{1,0:T(8,128)}) %reduce-scatter.2.cloned.1.call-update) | async-done | bytes 131088 | tf_op jit(solution)/shard_map/reduce_scatter | solution.py:55
  163.6 1.7 copy.22
  165.2 20.2 %all-to-all-start = ((f32[1,128,256]{2,0,1:T(1,128)}), f32[1,128,256]{2,0,1:T(1,128)S(1)}, u32[]{:S(2)}, u32[]{:S(2)}) async-start(f32[1,128,256]{2,0,1:T(1,128)} %copy.22), calls=%async_computation.1 | async-start | bytes 262144 | tf_op jit(solution)/shard_map/all_to_all | solution.py:58
  185.4 0.0 copy-done.2
  185.4 5.0 %fusion.18 = (bf16[1,1,128,768]{3,2,1,0:T(8,128)(2,1)S(1)}, bf16[1,1,128,768]{3,2,1,0:T(8,128)(2,1)S(1)}) fusion(f32[128,1536]{1,0:T(8,128)S(1)} %copy-done.2, bf16[128,4096]{1,0:T(8,128)(2,1)S(1)} %reshape.87, bf16[1,768,4096]{2,1,0:T(8,128)(2,1)} %param.15), kind=kOutput, calls=%fused_computation.35 | convolution fusion | flops 806584320 | bytes 8519680 | tf_op jit(solution)/shard_map/dot_general | solution.py:87
  190.5 0.8 pad_maximum_fusion.1
  191.2 5.3 %all-to-all-done = f32[1,128,256]{2,0,1:T(1,128)S(1)} async-done(((f32[1,128,256]{2,0,1:T(1,128)}), f32[1,128,256]{2,0,1:T(1,128)S(1)}, u32[]{:S(2)}, u32[]{:S(2)}) %all-to-all-start) | async-done | bytes 131104 | tf_op jit(solution)/shard_map/all_to_all | solution.py:58
  196.5 0.3 reduce
  196.8 0.1 reshape.85
  197.0 0.6 copy.23
  (7 shorter events, 0.1 us)
Async XLA Ops:
  7.2 1.0 copy-start
  7.2 79.9 %copy-start.4 = (bf16[128,128]{1,0:T(8,128)(2,1)S(1)}, bf16[128,128]{1,0:T(8,128)(2,1)}, u32[]{:S(2)}) copy-start(bf16[128,128]{1,0:T(8,128)(2,1)} %param.10) | copy-start | bytes 98308
  7.2 78.0 %all-gather.2.cloned.1.call-start = ((), (), s32[]{:S(2)}) async-start(), calls=%async_computation.3 | async-start | bytes 1114112 | tf_op jit(solution)/shard_map/all_gather | solution.py:23
  8.8 154.8 %reduce-scatter.2.cloned.1.call-start = ((), (), s32[]{:S(2)}) async-start(), calls=%async_computation.4 | async-start | bytes 2228224 | tf_op jit(solution)/shard_map/reduce_scatter | solution.py:55
  85.2 2.2 %copy-start.1 = (bf16[2,2048,128]{2,1,0:T(8,128)(2,1)S(1)}, bf16[2,2048,128]{2,1,0:T(8,128)(2,1)}, u32[]{:S(2)}) copy-start(bf16[2,2048,128]{2,1,0:T(8,128)(2,1)} %all-gather.2.cloned.1.call-done) | copy-start | bytes 3145732
  87.4 0.8 copy-start.7
  90.0 0.8 copy-start.5
  90.0 0.9 copy-start.8
  90.0 0.9 copy-start.6
  93.5 20.0 %copy-start.3 = (bf16[1,1,128,1536]{3,2,1,0:T(8,128)(2,1)S(1)}, bf16[1,1,128,1536]{3,2,1,0:T(8,128)(2,1)}, u32[]{:S(2)}) copy-start(bf16[1,1,128,1536]{3,2,1,0:T(8,128)(2,1)} %param.14) | copy-start | bytes 1179652
  93.5 48.0 %all-to-all-start.1 = ((bf16[64,2,4096]{2,1,0:T(2,128)(2,1)}), bf16[64,2,4096]{2,1,0:T(2,128)(2,1)S(1)}, u32[]{:S(2)}, u32[]{:S(2)}) async-start(bf16[64,2,4096]{2,1,0:T(2,128)(2,1)} %reshape.86), calls=%async_computation.2 | async-start | bytes 2097152 | tf_op jit(solution)/shard_map/all_to_all | solution.py:86
  115.4 70.0 %copy-start.2 = (f32[128,1536]{1,0:T(8,128)S(1)}, f32[128,1536]{1,0:T(8,128)}, u32[]{:S(2)}) copy-start(f32[128,1536]{1,0:T(8,128)} %bitcast_convert_fusion) | copy-start | bytes 2359300
  165.2 31.3 %all-to-all-start = ((f32[1,128,256]{2,0,1:T(1,128)}), f32[1,128,256]{2,0,1:T(1,128)S(1)}, u32[]{:S(2)}, u32[]{:S(2)}) async-start(f32[1,128,256]{2,0,1:T(1,128)} %copy.22), calls=%async_computation.1 | async-start | bytes 262144 | tf_op jit(solution)/shard_map/all_to_all | solution.py:58
Sparse Core Ops, SparseCore 0:
  11.3 73.9 all-gather.1
  90.2 73.3 reduce-scatter.1
where the time goes:
time: 205 us; the launch traced here: 204 us
  waiting for transfers between devices  129 us (63%)
  starting transfers between devices  40.2 us (20%)
  between operations  14.2 us (7%)
  matrix products  9.45 us (5%)
  local copies, waits for them, and re-layouts  7.65 us (4%)
  other arithmetic  4.3 us (2%)
    all_gather x1, waiting for transfers between devices, body(): all_pairs = lax.all_gather(own_pair, 'ctx', axis=1, tiled=True)  75.5 us
    all_to_all x1, waiting for transfers between devices, body(): lax.all_to_all(outgoing, 'exp', split_axis=0, concat_axis=0, tiled=True)  26.1 us
    reduce_scatter x1, waiting for transfers between devices, body(): lax.psum_scatter(jnp.concatenate([key_grad, value_grad], axis=1), 'ctx',...  21.7 us
    all_to_all x1, starting transfers between devices, body(): lax.all_to_all(key_grads.reshape(1, row_count, 2 * head_dim), 'exp', spli...  20.2 us
    all_to_all x1, starting transfers between devices, body(): lax.all_to_all(outgoing, 'exp', split_axis=0, concat_axis=0, tiled=True)  20 us
    all_to_all x1, waiting for transfers between devices, body(): lax.all_to_all(key_grads.reshape(1, row_count, 2 * head_dim), 'exp', spli...  5.28 us
    dot_general x1, matrix products, body(): lax.dot_general(incoming.reshape(exp_count * capacity, width), down_weigh...  5.05 us
  transfers between devices with their start and end apart: 4, of which 4 were waited for; matrix products, arithmetic and copies ran while one was open for 6% of the time, Pallas kernels for 0%

commit v1 on v0

v1 whole, which is shorter than its diff:
```python
import math

import jax
import jax.numpy as jnp
from jax import lax
from jax.experimental import pallas as pl
from jax.experimental.pallas import tpu as pltpu
from jax.sharding import PartitionSpec as P

MESH = pl.DeviceIdType.MESH
F32, BF16, I32 = jnp.float32, jnp.bfloat16, jnp.int32

NZ = 16
NE = 64
NX = 4
NY = 8
ROWS = 128
HEAD = 128
SUB = ROWS // NX
KEYS = NZ * SUB
HALF = SUB // 2
FF = 768
CH = 512
NQ = 8
MSG = 2 * NQ
SLOTS = 2 * NE
MASKED = -1e30

contract_last = (((1,), (1,)), ((), ()))
contract_first = (((0,), (0,)), ((), ()))


def send(src, dst, ss, rs, device):
    return pltpu.make_async_remote_copy(
        src_ref=src, dst_ref=dst, send_sem=ss, recv_sem=rs, device_id=device, device_id_type=MESH
    )


def route_matrix(ids_ref, wts_ref):
    ids = ids_ref[...].astype(F32)
    wts = wts_ref[...]
    col = lax.broadcasted_iota(I32, (8, 128), 1)
    tok = lax.broadcasted_iota(I32, (8, 128), 0)
    col_tok = lax.rem(col, 8)
    chunk = (lax.rem(col, 64) // 8)[0:1]
    low = col[0:1] >= 64
    pick = col_tok == tok
    earlier = tok < col_tok
    spread = []
    for k in range(8):
        spread.append(jnp.broadcast_to(ids[:, k : k + 1], (8, 128)))
    row = lax.broadcasted_iota(I32, (SLOTS * NQ, 128), 0)
    total = jnp.zeros((SLOTS * NQ, 128), F32)
    for k in range(8):
        named = jnp.sum(jnp.where(pick, spread[k], 0.0), axis=0, keepdims=True)
        weight = jnp.sum(
            jnp.where(pick, jnp.broadcast_to(wts[:, k : k + 1], (8, 128)), 0.0),
            axis=0,
            keepdims=True,
        )
        count = jnp.zeros((8, 128), F32)
        for other in range(8):
            count += jnp.where(earlier & (spread[other] == named), 1.0, 0.0)
        slot = jnp.sum(count, axis=0, keepdims=True)
        code = (named * (2 * NQ) + slot * NQ).astype(I32) + chunk
        high = weight.astype(BF16).astype(F32)
        part = jnp.where(low, weight - high, high)
        total += jnp.where(row == code, part, 0.0)
    return total.astype(BF16)


def kernel(
    q_ref, kv_ref, do_ref, tok_ref, ids_ref, wts_ref, saved_ref, down_ref,
    dq_out, dkv_out, dgu_out,
    qd, kv, pun, dps, stats, dqs, dqr, acc, halves, core_in, zs, zr, fs, fr,
    tok_v, ids_v, wts_v, saved_v, down_v, outgoing, incoming,
    loc, kv_ss, kv_rs, x_ss, x_rs, st_ss, st_rs, dq_ss, dq_rs, c_ss, c_rs,
    z_ss, z_rs, f_ss, f_rs, a_ss, a_rs,
):
    z, e = lax.axis_index("ctx"), lax.axis_index("exp")
    c = lax.rem(e, 2)
    x = lax.rem(e // 2, NX)
    y = e // (2 * NX)
    g = y // 2
    scale = 1.0 / math.sqrt(HEAD)
    partner = {"ctx": z, "exp": e + 1 - 2 * c}

    def x_peer(k):
        other = lax.rem(x + k, NX)
        return other, {"ctx": z, "exp": y * (2 * NX) + other * 2 + c}

    kv[...] = jnp.zeros_like(kv)
    zr[...] = jnp.zeros_like(zr)
    barrier = pltpu.get_barrier_semaphore()

    @pl.loop(1, NZ)
    def _(k):
        pl.semaphore_signal(
            barrier, inc=1, device_id={"ctx": lax.rem(z + k, NZ), "exp": e}, device_id_type=MESH
        )

    @pl.loop(1, NE)
    def _(k):
        pl.semaphore_signal(
            barrier, inc=1, device_id={"ctx": z, "exp": lax.rem(e + k, NE)}, device_id_type=MESH
        )

    local = [
        pltpu.make_async_copy(
            kv_ref.at[c, pl.ds(x * SUB, SUB), pl.ds(g * HEAD, HEAD)], kv.at[c, z], loc.at[0]
        ),
        pltpu.make_async_copy(q_ref, qd.at[x, 0], loc.at[1]),
        pltpu.make_async_copy(do_ref, qd.at[x, 1], loc.at[2]),
        pltpu.make_async_copy(tok_ref, tok_v, loc.at[3]),
        pltpu.make_async_copy(ids_ref, ids_v, loc.at[4]),
        pltpu.make_async_copy(wts_ref, wts_v, loc.at[5]),
        pltpu.make_async_copy(saved_ref.at[0, 0], saved_v, loc.at[6]),
        pltpu.make_async_copy(down_ref.at[0], down_v, loc.at[7]),
    ]
    for copy in local:
        copy.start()
    for copy in local[:6]:
        copy.wait()

    wide = tok_v[...].astype(F32)
    chunks = [wide[:, n * CH : (n + 1) * CH] for n in range(NQ)]
    tokens = jnp.concatenate(chunks + chunks, axis=0).astype(BF16)
    outgoing[...] = jnp.dot(
        route_matrix(ids_v, wts_v), tokens, preferred_element_type=F32
    ).astype(BF16)

    pl.semaphore_wait(barrier, NZ - 1 + NE - 1)

    @pl.loop(1, NZ)
    def _(k):
        to = NZ - k

        @pl.when(to > z)
        def _():
            send(
                kv.at[c, z], kv.at[c, z], kv_ss.at[to], kv_rs.at[z], {"ctx": to, "exp": e}
            ).start()

    x_sends = []
    for k in (2, 1, 3):
        _, device = x_peer(k)
        x_sends.append(send(qd.at[x], qd.at[x], x_ss.at[k], x_rs.at[x], device))
        x_sends[-1].start()

    @pl.loop(1, NE)
    def _(k):
        to = lax.rem(e + k, NE)
        send(
            outgoing.at[pl.ds(pl.multiple_of(to * MSG, MSG), MSG)],
            incoming.at[pl.ds(pl.multiple_of(e * MSG, MSG), MSG)],
            a_ss,
            a_rs,
            {"ctx": z, "exp": to},
        ).start()

    own_rows = pl.ds(pl.multiple_of(e * MSG, MSG), MSG)
    own_tokens = pltpu.make_async_copy(outgoing.at[own_rows], incoming.at[own_rows], loc.at[0])
    own_tokens.start()

    @pl.loop(0, NZ)
    def _(j):
        @pl.when(j < z)
        def _():
            send(kv.at[c, j], kv.at[c, j], kv_ss.at[j], kv_rs.at[j], partner).wait_recv()

    swap = send(kv.at[c], kv.at[c], c_ss.at[0], c_rs.at[0], partner)
    swap.start()
    for k in (1, 2, 3):
        other, device = x_peer(k)
        send(qd.at[other], qd.at[other], x_ss.at[k], x_rs.at[other], device).wait_recv()
    swap.wait_recv()

    keys = kv[0].reshape(KEYS, HEAD)
    values = kv[1].reshape(KEYS, HEAD)
    at = lax.broadcasted_iota(I32, (KEYS, ROWS), 0)
    key_pos = (at // SUB) * ROWS + x * SUB + lax.rem(at, SUB)
    query_pos = z * ROWS + lax.broadcasted_iota(I32, (KEYS, ROWS), 1)
    causal = key_pos <= query_pos
    stats[x, 12:16] = jnp.zeros((4, ROWS), F32)
    for h in range(NX):
        s = lax.dot_general(keys, qd[h, 0], contract_last, preferred_element_type=F32) * scale
        s = jnp.where(causal, s, MASKED)
        m = jnp.max(s, axis=0, keepdims=True)
        p = jnp.exp(s - m)
        d = lax.dot_general(values, qd[h, 1], contract_last, preferred_element_type=F32)
        pun[h] = p
        dps[h] = d
        stats[x, pl.ds(h, 1)] = m
        stats[x, pl.ds(4 + h, 1)] = jnp.sum(p, axis=0, keepdims=True)
        stats[x, pl.ds(8 + h, 1)] = jnp.sum(p * d, axis=0, keepdims=True)
    st_sends = []
    for k in (2, 1, 3):
        _, device = x_peer(k)
        st_sends.append(send(stats.at[x], stats.at[x], st_ss.at[k], st_rs.at[x], device))
        st_sends[-1].start()
    for k in (1, 2, 3):
        other, device = x_peer(k)
        send(stats.at[other], stats.at[other], st_ss.at[k], st_rs.at[other], device).wait_recv()

    highs = [stats[n, 0:4] for n in range(NX)]
    top = jnp.maximum(jnp.maximum(highs[0], highs[1]), jnp.maximum(highs[2], highs[3]))
    shifts = [jnp.exp(highs[n] - top) for n in range(NX)]
    mass = sum(stats[n, 4:8] * shifts[n] for n in range(NX))
    delta = sum(stats[n, 8:12] * shifts[n] for n in range(NX)) / mass
    factor = jnp.exp(stats[x, 0:4] - (top + jnp.log(mass)))

    keys_t = keys.astype(F32).T.astype(BF16)
    dk = jnp.zeros((KEYS, HEAD), F32)
    dv = jnp.zeros((KEYS, HEAD), F32)
    for h in range(NX):
        p = pun[h] * factor[h : h + 1]
        ds = (p * (dps[h] - delta[h : h + 1])).astype(BF16)
        dv += jnp.dot(p.astype(BF16), qd[h, 1], preferred_element_type=F32)
        dk += jnp.dot(ds, qd[h, 0], preferred_element_type=F32)
        dqs[h] = (jnp.dot(keys_t, ds, preferred_element_type=F32) * scale).astype(BF16)
    acc[:, 0:HEAD] = dk * scale
    acc[:, HEAD:] = dv
    grid = acc[...].reshape(NZ, 2, HALF, 2 * HEAD)
    for n in range(2):
        halves[n] = grid[:, n].astype(BF16)
    pair = send(halves.at[1 - c], core_in, c_ss.at[1], c_rs.at[1], partner)
    pair.start()
    dq_sends = []
    for k in (2, 1, 3):
        other, device = x_peer(k)
        dq_sends.append(send(dqs.at[other], dqr.at[x], dq_ss.at[k], dq_rs.at[x], device))
        dq_sends[-1].start()
    pair.wait_recv()
    zs[...] = (halves[c].astype(F32) + core_in[...].astype(F32)).astype(BF16)

    @pl.loop(0, NZ)
    def _(j):
        @pl.when(j < z)
        def _():
            send(zs.at[j], zr.at[z], z_ss.at[j], z_rs.at[z], {"ctx": j, "exp": e}).start()

    for copy in local[6:]:
        copy.wait()
    own_tokens.wait()
    most = pl.ds(0, (NE - 1) * MSG)
    pltpu.make_async_copy(incoming.at[most], incoming.at[most], a_rs).wait()
    hidden = jnp.zeros((SLOTS, FF), F32)
    slot = lax.broadcasted_iota(I32, (SLOTS, SLOTS * NQ), 0) * NQ
    place = lax.broadcasted_iota(I32, (SLOTS, SLOTS * NQ), 1)
    for n in range(NQ):
        take = jnp.where(place == slot + n, 1.0, 0.0).astype(BF16)
        part = jnp.dot(take, incoming[...], preferred_element_type=F32).astype(BF16)
        hidden += lax.dot_general(
            part, down_v[:, n * CH : (n + 1) * CH], contract_last, preferred_element_type=F32
        )
    gate = saved_v[:, :FF].astype(F32)
    up = saved_v[:, FF:].astype(F32)
    sig = 1.0 / (1.0 + jnp.exp(-gate))
    dgu_out[0, 0, :, :FF] = (hidden * up * sig * (1.0 + gate * (1.0 - sig))).astype(BF16)
    dgu_out[0, 0, :, FF:] = (hidden * gate * sig).astype(BF16)

    dq = dqs[x].astype(F32)
    for k in (1, 2, 3):
        other, device = x_peer(k)
        send(dqs.at[other], dqr.at[other], dq_ss.at[k], dq_rs.at[other], device).wait_recv()
        dq += dqr[other].astype(F32)
    dq_out[...] = dq.T.astype(BF16)

    @pl.loop(0, NZ)
    def _(j):
        @pl.when(j > z)
        def _():
            send(zs.at[j], zr.at[j], z_ss.at[j], z_rs.at[j], partner).wait_recv()

    summed = zs[z].astype(F32)
    for n in range(NZ):
        summed += zr[n].astype(F32)
    for n in range(8):
        fs[n] = summed[2 * n : 2 * n + 2]
    base = (2 * x + c) * 8
    for n in range(8):

        @pl.when(base + n != e)
        def _(n=n):
            send(fs.at[n], fr.at[y], f_ss.at[n], f_rs.at[y], {"ctx": z, "exp": base + n}).start()

        @pl.when(base + n == e)
        def _(n=n):
            fr[y] = fs[n]

    for n in range(NY):

        @pl.when(n * 8 + y != e)
        def _(n=n):
            send(fs.at[0], fr.at[n], f_ss.at[0], f_rs.at[n], partner).wait_recv()

    for n in range(4):
        dkv_out[:, n, :] = fr[2 * n] + fr[2 * n + 1]

    for copy in x_sends + st_sends + dq_sends + [swap, pair]:
        copy.wait_send()

    @pl.loop(0, NZ)
    def _(j):
        @pl.when(j > z)
        def _():
            send(kv.at[c, z], kv.at[c, z], kv_ss.at[j], kv_rs.at[j], partner).wait_send()

        @pl.when(j < z)
        def _():
            send(zs.at[j], zr.at[j], z_ss.at[j], z_rs.at[j], partner).wait_send()

    for n in range(8):

        @pl.when(base + n != e)
        def _(n=n):
            send(fs.at[n], fr.at[n], f_ss.at[n], f_rs.at[n], partner).wait_send()

    pltpu.make_async_copy(outgoing.at[most], outgoing.at[most], a_ss).wait()


def body(
    queries, keyvals, d_attn, grad_tokens, expert_ids, route_weights, saved_gate_up, down_weight
):
    dma = pltpu.SemaphoreType.DMA
    vmem = pltpu.VMEM
    return pl.pallas_call(
        kernel,
        out_shape=(
            jax.ShapeDtypeStruct((ROWS, HEAD), BF16),
            jax.ShapeDtypeStruct((2, 4, 2 * HEAD), F32),
            jax.ShapeDtypeStruct((1, 1, SLOTS, 2 * FF), BF16),
        ),
        in_specs=[pl.BlockSpec(memory_space=pltpu.HBM)] * 8,
        out_specs=tuple([pl.BlockSpec(memory_space=vmem)] * 3),
        scratch_shapes=[
            vmem((NX, 2, ROWS, HEAD), BF16),
            vmem((2, NZ, SUB, HEAD), BF16),
            vmem((NX, KEYS, ROWS), F32),
            vmem((NX, KEYS, ROWS), F32),
            vmem((NX, 16, ROWS), F32),
            vmem((NX, HEAD, ROWS), BF16),
            vmem((NX, HEAD, ROWS), BF16),
            vmem((KEYS, 2 * HEAD), F32),
            vmem((2, NZ, HALF, 2 * HEAD), BF16),
            vmem((NZ, HALF, 2 * HEAD), BF16),
            vmem((NZ, HALF, 2 * HEAD), BF16),
            vmem((NZ, HALF, 2 * HEAD), BF16),
            vmem((8, 2, 2 * HEAD), F32),
            vmem((NY, 2, 2 * HEAD), F32),
            vmem((8, NQ * CH), BF16),
            vmem((8, 8), I32),
            vmem((8, 8), F32),
            vmem((SLOTS, 2 * FF), BF16),
            vmem((FF, NQ * CH), BF16),
            vmem((SLOTS * NQ, CH), BF16),
            vmem((SLOTS * NQ, CH), BF16),
            dma((8,)),
            dma((NZ,)),
            dma((NZ,)),
            dma((4,)),
            dma((4,)),
            dma((4,)),
            dma((4,)),
            dma((4,)),
            dma((4,)),
            dma((2,)),
            dma((2,)),
            dma((NZ,)),
            dma((NZ,)),
            dma((8,)),
            dma((8,)),
            dma,
            dma,
        ],
        compiler_params=pltpu.CompilerParams(
            collective_id=0, has_side_effects=True, vmem_limit_bytes=60 * 1024 * 1024
        ),
        name="layer_backward",
    )(
        queries, keyvals, d_attn, grad_tokens, expert_ids, route_weights, saved_gate_up, down_weight
    )


def solution(mesh):
    placed = (
        P("ctx", "exp"),
        P(None, "ctx", None),
        P("ctx", "exp"),
        P(("ctx", "exp"), None),
        P(("ctx", "exp"), None),
        P(("ctx", "exp"), None),
        P("ctx", "exp", None, None),
        P("exp", None, None),
    )
    return jax.shard_map(
        body,
        mesh=mesh,
        in_specs=placed,
        out_specs=(P("ctx", "exp"), P(("ctx", "exp"), None, None), P("ctx", "exp", None, None)),
        check_vma=False,
    )
```

time: 205 us -> 62.9 us (0.31)
  waiting for transfers between devices: 129 us -> 0 us
  Pallas kernels: 0 us -> 57.4 us
  starting transfers between devices: 40.2 us -> 0 us
  between operations: 14.2 us -> 0.64 us
  matrix products: 9.45 us -> 0 us
  other arithmetic: 4.3 us -> 0 us
  local copies, waits for them, and re-layouts: 7.65 us -> 4.44 us
    all_gather x1 -> x0, waiting for transfers between devices: 75.5 us -> none  [body(): all_pairs = lax.all_gather(own_pair, 'ctx', axis=1, tiled=True)]
    pallas_call x0 -> x1, Pallas kernels: none -> 57.4 us  [body(): pl.pallas_call(kernel, out_shape=(jax.ShapeDtypeStruct((ROWS, HEAD), BF16...]
    all_to_all x2 -> x0, starting transfers between devices: 40.1 us -> none  [the longest x1 20.2 us: body(): lax.all_to_all(key_grads.reshape(1, row_count, 2 * head_dim), 'exp', spli...]
    all_to_all x2 -> x0, waiting for transfers between devices: 31.3 us -> none  [the longest x1 26.1 us: body(): lax.all_to_all(outgoing, 'exp', split_axis=0, concat_axis=0, tiled=True)]
    reduce_scatter x1 -> x0, waiting for transfers between devices: 21.7 us -> none  [body(): lax.psum_scatter(jnp.concatenate([key_grad, value_grad], axis=1), 'ctx',...]
    dot_general x8 -> x0, matrix products: 9.45 us -> none  [the longest x1 5.05 us: body(): lax.dot_general(incoming.reshape(exp_count * capacity, width), down_weigh...]
    reshape x4 -> x0, local copies, waits for them, and re-layouts: 3.68 us -> none  [the longest x1 1.68 us: body(): key_grads.reshape(1, row_count, 2 * head_dim)]
    concatenate x2 -> x0, other arithmetic: 2.26 us -> none  [the longest x1 1.49 us: body(): jnp.concatenate([key_grad, value_grad], axis=1)]
  transfers between devices with their start and end apart: 4 -> 0, of which waited for: 4 -> 0; matrix products, arithmetic and copies ran while one was open for 6% -> 0% of each run, Pallas kernels for 0% -> 0%
where the time goes in v1:
time: 62.9 us; the launch traced here: 62.5 us
  Pallas kernels  57.4 us (91%)
  local copies, waits for them, and re-layouts  4.44 us (7%)
  between operations  0.64 us (1%)
    pallas_call x1, Pallas kernels, body(): pl.pallas_call(kernel, out_shape=(jax.ShapeDtypeStruct((ROWS, HEAD), BF16...  57.4 us
    unnamed x3, local copies, waits for them, and re-layouts  4.44 us

profile of v1, /device:TPU:1, one launch (start us, length us, event | category | flops | bytes accessed | tf_op | source)
XLA Modules:
  0.0 62.5 jit_solution(4449233825496374618)
XLA Ops:
  0.6 57.4 %layer_backward.1 = (bf16[128,128]{1,0:T(8,128)(2,1)}, f32[2,4,256]{2,1,0:T(4,128)}, bf16[1,1,128,1536]{3,2,1,0:T(8,128)(2,1)}) custom-call(bf16[128,128]{1,0:T(8,128)(2,1)} %q_ref.1, bf16[2,128,512]{2,1,0:T(8,128)(2,1)} %kv_ref.1, bf16[128,128]{1,0:T(8,128)(2,1)} %do_ref.1, bf16[8,4096]{1,0:T(8,128)(2,1)} %tok_ref.1, s32[8,8]{1,0:T(8,128)} %ids_ref.1, ...), custom_call_target="tpu_custom_call" | custom-call | tf_op jit(solution)/shard_map/layer_backward/pallas_call | solution.py:327
  58.1 1.4 %copy.14 = bf16[128,128]{1,0:T(8,128)(2,1)} copy(bf16[128,128]{1,0:T(8,128)(2,1)} %get-tuple-element.6) | data formatting | bytes 65536
  59.4 1.3 %copy.15 = f32[2,4,256]{2,1,0:T(4,128)} copy(f32[2,4,256]{2,1,0:T(4,128)} %get-tuple-element.7) | data formatting | bytes 16384
  60.7 1.8 %copy.16 = bf16[1,1,128,1536]{3,2,1,0:T(8,128)(2,1)} copy(bf16[1,1,128,1536]{3,2,1,0:T(8,128)(2,1)} %get-tuple-element.8) | data formatting | bytes 786432

commit v2 on v0

v2 whole, which is shorter than its diff:
```python
import math

import jax
import jax.numpy as jnp
from jax import lax
from jax.experimental import pallas as pl
from jax.experimental.pallas import tpu as pltpu
from jax.sharding import PartitionSpec as P

MESH = pl.DeviceIdType.MESH
F32, BF16, I32 = jnp.float32, jnp.bfloat16, jnp.int32

NZ = 16
NP = 8
ROWS = 128
HEAD = 128
SUB = ROWS // NP
KEYS = NZ * SUB
QUERIES = NP * ROWS
FF = 768
WIDTH = 4096
SIDE = WIDTH // 2
EXTRA = 128
CUT = SIDE // 2
SLOTS = 128
MASKED = -1e30

contract_last = (((1,), (1,)), ((), ()))


def send(src, dst, ss, rs, device):
    return pltpu.make_async_remote_copy(
        src_ref=src, dst_ref=dst, send_sem=ss, recv_sem=rs, device_id=device, device_id_type=MESH
    )


def choices(ids, weights):
    ids = ids.astype(F32)
    token = lax.broadcasted_iota(I32, (8, 8), 0)
    slot = jnp.zeros((8, 8), F32)
    for t in range(7):
        for k in range(8):
            slot += jnp.where((ids[t : t + 1, k : k + 1] == ids) & (token > t), 1.0, 0.0)
    high = weights.astype(BF16)
    low = (weights - high.astype(F32)).astype(BF16)
    at = lax.broadcasted_iota(I32, (8, EXTRA), 1) - lax.broadcasted_iota(I32, (8, EXTRA), 0)
    out = jnp.zeros((8, EXTRA), F32)
    for n, part in enumerate(((ids * 2.0 + slot).astype(BF16), high, low)):
        spread = jnp.where(at == 8 * n, 1.0, 0.0).astype(BF16)
        out += jnp.dot(part, spread, preferred_element_type=F32)
    return out


def kernel(
    q_ref, kv_ref, do_ref, tok_ref, ids_ref, wts_ref, saved_ref, down_ref,
    dq_out, dkv_out, dgu_out,
    block, kv, qd, pun, dps, pb, sb, stats, dqs, dqr, zs, zr, fs, fr,
    tok_v, ids_v, wts_v, saved_v, down_v, tb, outgoing, incoming,
    loc, kv_ss, kv_rs, x_ss, x_rs, st_ss, st_rs, dq_ss, dq_rs,
    z_ss, z_rs, f_ss, f_rs, t_ss, t_rs, a_ss, a_rs,
):
    z, e = lax.axis_index("ctx"), lax.axis_index("exp")
    d = lax.rem(e, NP)
    y = e // NP
    g = y // 2
    scale = 1.0 / math.sqrt(HEAD)

    def row(k):
        other = lax.rem(d + k, NP)
        return other, {"ctx": z, "exp": y * NP + other}

    def column(k):
        other = lax.rem(y + k, NP)
        return other, {"ctx": z, "exp": other * NP + d}

    partner = {"ctx": z, "exp": e + 1 - 2 * lax.rem(e, 2)}
    order = (4, 5, 3, 2, 6, 7, 1)
    cuts = (pl.ds(0, EXTRA + CUT), pl.ds(EXTRA + CUT, CUT))
    own = pl.ds(pl.multiple_of(d * 16, 16), 16)

    local = [
        pltpu.make_async_copy(kv_ref.at[:, :, pl.ds(g * HEAD, HEAD)], block, loc.at[0]),
        pltpu.make_async_copy(q_ref, qd.at[0, d], loc.at[1]),
        pltpu.make_async_copy(do_ref, qd.at[1, d], loc.at[2]),
        pltpu.make_async_copy(tok_ref, tok_v, loc.at[3]),
        pltpu.make_async_copy(ids_ref, ids_v, loc.at[4]),
        pltpu.make_async_copy(wts_ref, wts_v, loc.at[5]),
        pltpu.make_async_copy(saved_ref.at[0, 0], saved_v, loc.at[6]),
        pltpu.make_async_copy(down_ref.at[0], down_v, loc.at[7]),
    ]
    for copy in local:
        copy.start()

    kv[...] = jnp.zeros_like(kv)
    zr[...] = jnp.zeros_like(zr)
    barrier = pltpu.get_barrier_semaphore()

    @pl.loop(1, NZ)
    def _(k):
        pl.semaphore_signal(
            barrier, inc=1, device_id={"ctx": lax.rem(z + k, NZ), "exp": e}, device_id_type=MESH
        )

    for k in range(1, NP):
        for _, device in (row(k), column(k)):
            pl.semaphore_signal(barrier, inc=1, device_id=device, device_id_type=MESH)

    local[0].wait()
    near = lax.broadcasted_iota(I32, (SUB, ROWS), 0)
    far = lax.broadcasted_iota(I32, (SUB, ROWS), 1)
    chosen = (far == (near // 2) * SUB + 2 * d + lax.rem(near, 2)).astype(F32).astype(BF16)
    for n in range(2):
        kv[z, n] = jnp.dot(chosen, block[n], preferred_element_type=F32).astype(BF16)

    for copy in local[3:6]:
        copy.wait()
    wide = tok_v[...].astype(F32)
    tb[y, :, EXTRA:] = jnp.concatenate([wide[:, :SIDE], wide[:, SIDE:]], axis=0).astype(BF16)
    beside = choices(ids_v[...], wts_v[...])
    tb[y, :, :EXTRA] = jnp.concatenate([beside, beside], axis=0).astype(BF16)
    for copy in local[1:3]:
        copy.wait()

    pl.semaphore_wait(barrier, NZ - 1 + 2 * (NP - 1))

    @pl.loop(1, NZ)
    def _(k):
        to = NZ - k

        @pl.when(to > z)
        def _():
            send(kv.at[z], kv.at[z], kv_ss.at[to], kv_rs.at[z], {"ctx": to, "exp": e}).start()

    sends = []

    def start(copy):
        copy.start()
        sends.append(copy)

    for k in order:
        _, device = row(k)
        start(send(qd.at[:, d], qd.at[:, d], x_ss.at[k], x_rs.at[d], device))
    for n, cut in enumerate(cuts):
        for k in order:
            _, device = column(k)
            mine = tb.at[y, :, cut]
            start(send(mine, mine, t_ss.at[n, k], t_rs.at[n, y], device))

    for k in range(1, NP):
        other, _ = row(k)
        send(qd.at[:, other], qd.at[:, other], x_ss.at[k], x_rs.at[other], partner).wait_recv()

    @pl.loop(0, NZ)
    def _(j):
        @pl.when(j < z)
        def _():
            send(kv.at[j], kv.at[j], kv_ss.at[j], kv_rs.at[j], partner).wait_recv()

    keys = kv[:, 0].reshape(KEYS, HEAD)
    values = kv[:, 1].reshape(KEYS, HEAD)
    at = lax.broadcasted_iota(I32, (KEYS, ROWS), 0)
    in_block = lax.rem(at, SUB)
    key_pos = (at // SUB) * ROWS + (in_block // 2) * SUB + 2 * d + lax.rem(in_block, 2)
    causal = key_pos <= z * ROWS + lax.broadcasted_iota(I32, (KEYS, ROWS), 1)
    for h in range(NP):
        s = lax.dot_general(keys, qd[0, h], contract_last, preferred_element_type=F32) * scale
        s = jnp.where(causal, s, MASKED)
        m = jnp.max(s, axis=0, keepdims=True)
        p = jnp.exp(s - m)
        v = lax.dot_general(values, qd[1, h], contract_last, preferred_element_type=F32)
        pun[h] = p
        dps[h] = v
        stats[d, pl.ds(h, 1)] = m
        stats[d, pl.ds(NP + h, 1)] = jnp.sum(p, axis=0, keepdims=True)
        stats[d, pl.ds(2 * NP + h, 1)] = jnp.sum(p * v, axis=0, keepdims=True)
    for k in order:
        _, device = row(k)
        start(send(stats.at[d], stats.at[d], st_ss.at[k], st_rs.at[d], device))

    def await_tokens(n):
        for k in range(1, NP):
            other, _ = column(k)
            theirs = tb.at[other, :, cuts[n]]
            send(theirs, theirs, t_ss.at[n, k], t_rs.at[n, other], partner).wait_recv()

    await_tokens(0)
    beside = tb[:, :, :EXTRA].reshape(SLOTS, EXTRA).astype(F32).T
    r = lax.broadcasted_iota(I32, (SLOTS, SLOTS), 0)
    q = lax.broadcasted_iota(I32, (SLOTS, SLOTS), 1)
    wanted = ((y * NP + r // 16) * 2 + lax.rem(r, 2)).astype(F32)
    same = lax.rem(r, 16) // 2 == q // 16
    high = jnp.zeros((SLOTS, SLOTS), F32)
    low = jnp.zeros((SLOTS, SLOTS), F32)
    for k in range(8):
        hit = same & (beside[k : k + 1] == wanted)
        high += jnp.where(hit, beside[8 + k : 9 + k], 0.0)
        low += jnp.where(hit, beside[16 + k : 17 + k], 0.0)
    first = lax.rem(q, 16) < 8
    placers = [
        [jnp.where(first, part, 0.0).astype(BF16), jnp.where(first, 0.0, part).astype(BF16)]
        for part in (high, low)
    ]

    def pack(n):
        for half in range(2):
            for m in range(2):
                at = EXTRA + n * CUT + m * 512
                part = tb[:, :, at : at + 512].reshape(SLOTS, 512)
                outgoing[n, :, half * CUT + m * 512 : half * CUT + (m + 1) * 512] = (
                    jnp.dot(placers[0][half], part, preferred_element_type=F32)
                    + jnp.dot(placers[1][half], part, preferred_element_type=F32)
                ).astype(BF16)
        for k in order:
            other, device = row(k)
            theirs = pl.ds(pl.multiple_of(other * 16, 16), 16)
            start(
                send(
                    outgoing.at[n, theirs], incoming.at[n, own], a_ss.at[n, k], a_rs.at[n, d], device
                )
            )
        keep = pltpu.make_async_copy(outgoing.at[n, own], incoming.at[n, own], loc.at[n])
        keep.start()
        return keep

    own_tokens = [pack(0)]

    for k in range(1, NP):
        other, _ = row(k)
        send(stats.at[other], stats.at[other], st_ss.at[k], st_rs.at[other], partner).wait_recv()

    top = stats[0, 0:NP]
    for n in range(1, NP):
        top = jnp.maximum(top, stats[n, 0:NP])
    shifts = [jnp.exp(stats[n, 0:NP] - top) for n in range(NP)]
    mass = sum(stats[n, NP : 2 * NP] * shifts[n] for n in range(NP))
    delta = sum(stats[n, 2 * NP : 3 * NP] * shifts[n] for n in range(NP)) / mass
    factor = jnp.exp(stats[d, 0:NP] - (top + jnp.log(mass)))
    for h in range(NP):
        p = pun[h] * factor[h : h + 1]
        pb[:, h * ROWS : (h + 1) * ROWS] = p.astype(BF16)
        sb[:, h * ROWS : (h + 1) * ROWS] = (p * (dps[h] - delta[h : h + 1])).astype(BF16)
    dk = jnp.dot(sb[...], qd[0].reshape(QUERIES, HEAD), preferred_element_type=F32) * scale
    zs[:, :, :HEAD] = dk.astype(BF16).reshape(NZ, SUB, HEAD)
    dv = jnp.dot(pb[...], qd[1].reshape(QUERIES, HEAD), preferred_element_type=F32)
    zs[:, :, HEAD:] = dv.astype(BF16).reshape(NZ, SUB, HEAD)

    @pl.loop(0, NZ)
    def _(j):
        @pl.when(j < z)
        def _():
            send(zs.at[j], zr.at[z], z_ss.at[j], z_rs.at[z], {"ctx": j, "exp": e}).start()

    await_tokens(1)
    own_tokens.append(pack(1))

    keys_t = keys.astype(F32).T.astype(BF16)
    for h in range(NP):
        dqs[h] = (
            jnp.dot(keys_t, sb[:, h * ROWS : (h + 1) * ROWS], preferred_element_type=F32) * scale
        ).astype(BF16)
    for k in order:
        other, device = row(k)
        start(send(dqs.at[other], dqr.at[d], dq_ss.at[k], dq_rs.at[d], device))

    for copy in local[6:]:
        copy.wait()
    swap = (lax.rem(r, 16) // 2 == q // 16) & (r // 16 == lax.rem(q, 16) // 2)
    swap = (swap & (lax.rem(r, 2) == lax.rem(q, 2))).astype(F32).astype(BF16)

    def down_part(n):
        own_tokens[n].wait()
        for k in range(1, NP):
            other, _ = row(k)
            theirs = pl.ds(pl.multiple_of(other * 16, 16), 16)
            send(
                outgoing.at[n, own], incoming.at[n, theirs], a_ss.at[n, k], a_rs.at[n, other], partner
            ).wait_recv()
        total = jnp.zeros((SLOTS, FF), F32)
        for half in range(2):
            part = incoming[n, :, half * CUT : (half + 1) * CUT]
            rows = jnp.dot(swap, part, preferred_element_type=F32).astype(BF16)
            at = half * SIDE + n * CUT
            total += lax.dot_general(
                rows, down_v[:, at : at + CUT], contract_last, preferred_element_type=F32
            )
        return total

    hidden = down_part(0)

    @pl.loop(0, NZ)
    def _(j):
        @pl.when(j > z)
        def _():
            send(zs.at[j], zr.at[j], z_ss.at[j], z_rs.at[j], partner).wait_recv()

    summed = zs[z].astype(F32)
    for n in range(NZ):
        summed += zr[n].astype(F32)
    for n in range(NP):
        fs[n] = summed[2 * n : 2 * n + 2]
    fr[y] = fs[y]
    for k in range(1, NP):
        other, device = column(k)
        start(send(fs.at[other], fr.at[y], f_ss.at[k], f_rs.at[y], device))

    dq = dqs[d].astype(F32)
    for k in range(1, NP):
        other, _ = row(k)
        send(dqs.at[other], dqr.at[other], dq_ss.at[k], dq_rs.at[other], partner).wait_recv()
        dq += dqr[other].astype(F32)
    dq_out[...] = dq.T.astype(BF16)

    hidden += down_part(1)
    gate = saved_v[:, :FF].astype(F32)
    up = saved_v[:, FF:].astype(F32)
    sig = 1.0 / (1.0 + jnp.exp(-gate))
    dgu_out[0, 0, :, :FF] = (hidden * up * sig * (1.0 + gate * (1.0 - sig))).astype(BF16)
    dgu_out[0, 0, :, FF:] = (hidden * gate * sig).astype(BF16)

    for k in range(1, NP):
        other, _ = column(k)
        send(fs.at[other], fr.at[other], f_ss.at[k], f_rs.at[other], partner).wait_recv()
    for n in range(4):
        dkv_out[:, n, :] = fr[2 * n] + fr[2 * n + 1]

    for copy in sends:
        copy.wait_send()

    @pl.loop(0, NZ)
    def _(j):
        @pl.when(j > z)
        def _():
            send(kv.at[z], kv.at[z], kv_ss.at[j], kv_rs.at[j], partner).wait_send()

        @pl.when(j < z)
        def _():
            send(zs.at[j], zr.at[j], z_ss.at[j], z_rs.at[j], partner).wait_send()


def store_kernel(a_ref, b_ref, c_ref, a_out, b_out, c_out, sems):
    copies = [
        pltpu.make_async_copy(src, dst, sems.at[n])
        for n, (src, dst) in enumerate(((c_ref, c_out), (a_ref, a_out), (b_ref, b_out)))
    ]
    for copy in copies:
        copy.start()
    for copy in copies:
        copy.wait()


def body(
    queries, keyvals, d_attn, grad_tokens, expert_ids, route_weights, saved_gate_up, down_weight
):
    dma = pltpu.SemaphoreType.DMA
    vmem = pltpu.VMEM
    shapes = (
        jax.ShapeDtypeStruct((ROWS, HEAD), BF16),
        jax.ShapeDtypeStruct((2, 4, 2 * HEAD), F32),
        jax.ShapeDtypeStruct((1, 1, SLOTS, 2 * FF), BF16),
    )
    outs = pl.pallas_call(
        kernel,
        out_shape=shapes,
        in_specs=[pl.BlockSpec(memory_space=pl.ANY)] * 8,
        out_specs=tuple([pl.BlockSpec(memory_space=vmem)] * 3),
        scratch_shapes=[
            vmem((2, ROWS, HEAD), BF16),
            vmem((NZ, 2, SUB, HEAD), BF16),
            vmem((2, NP, ROWS, HEAD), BF16),
            vmem((NP, KEYS, ROWS), F32),
            vmem((NP, KEYS, ROWS), F32),
            vmem((KEYS, QUERIES), BF16),
            vmem((KEYS, QUERIES), BF16),
            vmem((NP, 3 * NP, ROWS), F32),
            vmem((NP, HEAD, ROWS), BF16),
            vmem((NP, HEAD, ROWS), BF16),
            vmem((NZ, SUB, 2 * HEAD), BF16),
            vmem((NZ, SUB, 2 * HEAD), BF16),
            vmem((NP, 2, 2 * HEAD), F32),
            vmem((NP, 2, 2 * HEAD), F32),
            vmem((8, WIDTH), BF16),
            vmem((8, 8), I32),
            vmem((8, 8), F32),
            vmem((SLOTS, 2 * FF), BF16),
            vmem((FF, WIDTH), BF16),
            vmem((NP, 16, SIDE + EXTRA), BF16),
            vmem((2, SLOTS, SIDE), BF16),
            vmem((2, SLOTS, SIDE), BF16),
            dma((8,)),
        ]
        + [dma((n,)) for n in (NZ, NZ, NP, NP, NP, NP, NP, NP, NZ, NZ, NP, NP)]
        + [dma((2, NP))] * 4,
        compiler_params=pltpu.CompilerParams(
            collective_id=0, has_side_effects=True, vmem_limit_bytes=60 * 1024 * 1024
        ),
        name="layer_backward",
    )(
        queries, keyvals, d_attn, grad_tokens, expert_ids, route_weights, saved_gate_up, down_weight
    )
    return pl.pallas_call(
        store_kernel,
        out_shape=shapes,
        in_specs=[pl.BlockSpec(memory_space=vmem)] * 3,
        out_specs=tuple([pl.BlockSpec(memory_space=pl.ANY)] * 3),
        scratch_shapes=[dma((3,))],
        name="store",
    )(*outs)


def solution(mesh):
    placed = (
        P("ctx", "exp"),
        P(None, "ctx", None),
        P("ctx", "exp"),
        P(("ctx", "exp"), None),
        P(("ctx", "exp"), None),
        P(("ctx", "exp"), None),
        P("ctx", "exp", None, None),
        P("exp", None, None),
    )
    return jax.shard_map(
        body,
        mesh=mesh,
        in_specs=placed,
        out_specs=(P("ctx", "exp"), P(("ctx", "exp"), None, None), P("ctx", "exp", None, None)),
        check_vma=False,
    )
```

time: 205 us -> 56.3 us (0.27)
  the two profiles are of different devices: /device:TPU:1 before, /device:TPU:64 now
where the time goes in v2:
time: 56.3 us; the launch traced here: 56.2 us
  Pallas kernels  55.5 us (99%)
  between operations  0.64 us (1%)
    pallas_call x1, Pallas kernels, body(): pl.pallas_call(kernel, out_shape=shapes, in_specs=[pl.BlockSpec(memory_sp...  53.7 us
    pallas_call x1, Pallas kernels, body(): pl.pallas_call(store_kernel, out_shape=shapes, in_specs=[pl.BlockSpec(mem...  1.81 us

profile of v2, /device:TPU:64, one launch (start us, length us, event | category | flops | bytes accessed | tf_op | source)
XLA Modules:
  0.0 56.2 jit_solution(12416650659941100517)
XLA Ops:
  0.6 53.7 %layer_backward.1 = (bf16[128,128]{1,0:T(8,128)(2,1)}, f32[2,4,256]{2,1,0:T(4,128)}, bf16[1,1,128,1536]{3,2,1,0:T(8,128)(2,1)}) custom-call(bf16[128,128]{1,0:T(8,128)(2,1)} %q_ref.1, bf16[2,128,512]{2,1,0:T(8,128)(2,1)} %kv_ref.1, bf16[128,128]{1,0:T(8,128)(2,1)} %do_ref.1, bf16[8,4096]{1,0:T(8,128)(2,1)} %tok_ref.1, s32[8,8]{1,0:T(8,128)} %ids_ref.1, ...), custom_call_target="tpu_custom_call" | custom-call | tf_op jit(solution)/shard_map/layer_backward/pallas_call | solution.py:361
  54.4 1.8 %store.1 = (bf16[128,128]{1,0:T(8,128)(2,1)}, f32[2,4,256]{2,1,0:T(4,128)}, bf16[1,1,128,1536]{3,2,1,0:T(8,128)(2,1)}) custom-call(bf16[128,128]{1,0:T(8,128)(2,1)} %get-tuple-element.6.a_ref, f32[2,4,256]{2,1,0:T(4,128)} %get-tuple-element.7.b_ref, bf16[1,1,128,1536]{3,2,1,0:T(8,128)(2,1)} %get-tuple-element.8.c_ref), custom_call_target="tpu_custom_call" | custom-call | tf_op jit(solution)/shard_map/store/pallas_call | solution.py:400

commit v3 on v2

--- a/solution.py
+++ b/solution.py
@@ -24,6 +24,7 @@
 CUT = SIDE // 2
 SLOTS = 128
 MASKED = -1e30
+LATE = 8
 
 contract_last = (((1,), (1,)), ((), ()))
 
@@ -53,9 +54,9 @@
 
 def kernel(
     q_ref, kv_ref, do_ref, tok_ref, ids_ref, wts_ref, saved_ref, down_ref,
-    dq_out, dkv_out, dgu_out,
-    block, kv, qd, pun, dps, pb, sb, stats, dqs, dqr, zs, zr, fs, fr,
-    tok_v, ids_v, wts_v, saved_v, down_v, tb, outgoing, incoming,
+    dq_hbm, dkv_hbm, dgu_hbm,
+    dq_out, dkv_out, dgu_out, block, kv, qd, pun, dps, pb, sb, stats, dqs, dqr, zs, zr, fs, fr,
+    tok_v, ids_v, wts_v, saved_v, down_v, tb, placers, outgoing, incoming,
     loc, kv_ss, kv_rs, x_ss, x_rs, st_ss, st_rs, dq_ss, dq_rs,
     z_ss, z_rs, f_ss, f_rs, t_ss, t_rs, a_ss, a_rs,
 ):
@@ -77,6 +78,19 @@
     order = (4, 5, 3, 2, 6, 7, 1)
     cuts = (pl.ds(0, EXTRA + CUT), pl.ds(EXTRA + CUT, CUT))
     own = pl.ds(pl.multiple_of(d * 16, 16), 16)
+
+    kv[...] = jnp.zeros_like(kv)
+    zr[...] = jnp.zeros_like(zr)
+    barrier = pltpu.get_barrier_semaphore()
+
+    @pl.loop(0, NZ - 1)
+    def _(k):
+        at = lax.rem(z + 8 + k + k // 8, NZ)
+        pl.semaphore_signal(barrier, inc=1, device_id={"ctx": at, "exp": e}, device_id_type=MESH)
+
+    for k in range(1, NP):
+        for _, device in (row(k), column(k)):
+            pl.semaphore_signal(barrier, inc=1, device_id=device, device_id_type=MESH)
 
     local = [
         pltpu.make_async_copy(kv_ref.at[:, :, pl.ds(g * HEAD, HEAD)], block, loc.at[0]),
@@ -91,20 +105,6 @@
     for copy in local:
         copy.start()
 
-    kv[...] = jnp.zeros_like(kv)
-    zr[...] = jnp.zeros_like(zr)
-    barrier = pltpu.get_barrier_semaphore()
-
-    @pl.loop(1, NZ)
-    def _(k):
-        pl.semaphore_signal(
-            barrier, inc=1, device_id={"ctx": lax.rem(z + k, NZ), "exp": e}, device_id_type=MESH
-        )
-
-    for k in range(1, NP):
-        for _, device in (row(k), column(k)):
-            pl.semaphore_signal(barrier, inc=1, device_id=device, device_id_type=MESH)
-
     local[0].wait()
     near = lax.broadcasted_iota(I32, (SUB, ROWS), 0)
     far = lax.broadcasted_iota(I32, (SUB, ROWS), 1)
@@ -125,9 +125,9 @@
 
     @pl.loop(1, NZ)
     def _(k):
-        to = NZ - k
-
-        @pl.when(to > z)
+        to = z + jnp.where(k <= 8, 9 - k, k)
+
+        @pl.when(to < NZ)
         def _():
             send(kv.at[z], kv.at[z], kv_ss.at[to], kv_rs.at[z], {"ctx": to, "exp": e}).start()
 
@@ -140,11 +140,15 @@
     for k in order:
         _, device = row(k)
         start(send(qd.at[:, d], qd.at[:, d], x_ss.at[k], x_rs.at[d], device))
-    for n, cut in enumerate(cuts):
-        for k in order:
-            _, device = column(k)
-            mine = tb.at[y, :, cut]
-            start(send(mine, mine, t_ss.at[n, k], t_rs.at[n, y], device))
+    def send_tokens():
+        for n, cut in enumerate(cuts):
+            for k in order:
+                _, device = column(k)
+                mine = tb.at[y, :, cut]
+                send(mine, mine, t_ss.at[n, k], t_rs.at[n, y], device).start()
+
+    late = z >= LATE
+    pl.when(jnp.logical_not(late))(send_tokens)
 
     for k in range(1, NP):
         other, _ = row(k)
@@ -183,23 +187,8 @@
             theirs = tb.at[other, :, cuts[n]]
             send(theirs, theirs, t_ss.at[n, k], t_rs.at[n, other], partner).wait_recv()
 
-    await_tokens(0)
-    beside = tb[:, :, :EXTRA].reshape(SLOTS, EXTRA).astype(F32).T
     r = lax.broadcasted_iota(I32, (SLOTS, SLOTS), 0)
     q = lax.broadcasted_iota(I32, (SLOTS, SLOTS), 1)
-    wanted = ((y * NP + r // 16) * 2 + lax.rem(r, 2)).astype(F32)
-    same = lax.rem(r, 16) // 2 == q // 16
-    high = jnp.zeros((SLOTS, SLOTS), F32)
-    low = jnp.zeros((SLOTS, SLOTS), F32)
-    for k in range(8):
-        hit = same & (beside[k : k + 1] == wanted)
-        high += jnp.where(hit, beside[8 + k : 9 + k], 0.0)
-        low += jnp.where(hit, beside[16 + k : 17 + k], 0.0)
-    first = lax.rem(q, 16) < 8
-    placers = [
-        [jnp.where(first, part, 0.0).astype(BF16), jnp.where(first, 0.0, part).astype(BF16)]
-        for part in (high, low)
-    ]
 
     def pack(n):
         for half in range(2):
@@ -207,22 +196,37 @@
                 at = EXTRA + n * CUT + m * 512
                 part = tb[:, :, at : at + 512].reshape(SLOTS, 512)
                 outgoing[n, :, half * CUT + m * 512 : half * CUT + (m + 1) * 512] = (
-                    jnp.dot(placers[0][half], part, preferred_element_type=F32)
-                    + jnp.dot(placers[1][half], part, preferred_element_type=F32)
+                    jnp.dot(placers[0, half], part, preferred_element_type=F32)
+                    + jnp.dot(placers[1, half], part, preferred_element_type=F32)
                 ).astype(BF16)
         for k in order:
             other, device = row(k)
             theirs = pl.ds(pl.multiple_of(other * 16, 16), 16)
-            start(
+            (
                 send(
                     outgoing.at[n, theirs], incoming.at[n, own], a_ss.at[n, k], a_rs.at[n, d], device
                 )
-            )
-        keep = pltpu.make_async_copy(outgoing.at[n, own], incoming.at[n, own], loc.at[n])
-        keep.start()
-        return keep
-
-    own_tokens = [pack(0)]
+            ).start()
+        pltpu.make_async_copy(outgoing.at[n, own], incoming.at[n, own], loc.at[n]).start()
+
+    def first_part():
+        await_tokens(0)
+        beside = tb[:, :, :EXTRA].reshape(SLOTS, EXTRA).astype(F32).T
+        wanted = ((y * NP + r // 16) * 2 + lax.rem(r, 2)).astype(F32)
+        same = lax.rem(r, 16) // 2 == q // 16
+        high = jnp.zeros((SLOTS, SLOTS), F32)
+        low = jnp.zeros((SLOTS, SLOTS), F32)
+        for k in range(8):
+            hit = same & (beside[k : k + 1] == wanted)
+            high += jnp.where(hit, beside[8 + k : 9 + k], 0.0)
+            low += jnp.where(hit, beside[16 + k : 17 + k], 0.0)
+        first = lax.rem(q, 16) < 8
+        for n, part in enumerate((high, low)):
+            placers[n, 0] = jnp.where(first, part, 0.0).astype(BF16)
+            placers[n, 1] = jnp.where(first, 0.0, part).astype(BF16)
+        pack(0)
+
+    pl.when(jnp.logical_not(late))(first_part)
 
     for k in range(1, NP):
         other, _ = row(k)
@@ -250,8 +254,7 @@
         def _():
             send(zs.at[j], zr.at[z], z_ss.at[j], z_rs.at[z], {"ctx": j, "exp": e}).start()
 
-    await_tokens(1)
-    own_tokens.append(pack(1))
+    pl.when(late)(send_tokens)
 
     keys_t = keys.astype(F32).T.astype(BF16)
     for h in range(NP):
@@ -262,13 +265,17 @@
         other, device = row(k)
         start(send(dqs.at[other], dqr.at[d], dq_ss.at[k], dq_rs.at[d], device))
 
+    pl.when(late)(first_part)
+    await_tokens(1)
+    pack(1)
+
     for copy in local[6:]:
         copy.wait()
     swap = (lax.rem(r, 16) // 2 == q // 16) & (r // 16 == lax.rem(q, 16) // 2)
     swap = (swap & (lax.rem(r, 2) == lax.rem(q, 2))).astype(F32).astype(BF16)
 
     def down_part(n):
-        own_tokens[n].wait()
+        pltpu.make_async_copy(outgoing.at[n, own], incoming.at[n, own], loc.at[n]).wait()
         for k in range(1, NP):
             other, _ = row(k)
             theirs = pl.ds(pl.multiple_of(other * 16, 16), 16)
@@ -309,22 +316,37 @@
         send(dqs.at[other], dqr.at[other], dq_ss.at[k], dq_rs.at[other], partner).wait_recv()
         dq += dqr[other].astype(F32)
     dq_out[...] = dq.T.astype(BF16)
+    written = [pltpu.make_async_copy(dq_out, dq_hbm, loc.at[2])]
+    written[-1].start()
 
     hidden += down_part(1)
     gate = saved_v[:, :FF].astype(F32)
     up = saved_v[:, FF:].astype(F32)
     sig = 1.0 / (1.0 + jnp.exp(-gate))
-    dgu_out[0, 0, :, :FF] = (hidden * up * sig * (1.0 + gate * (1.0 - sig))).astype(BF16)
-    dgu_out[0, 0, :, FF:] = (hidden * gate * sig).astype(BF16)
+    dgu_out[:, :FF] = (hidden * up * sig * (1.0 + gate * (1.0 - sig))).astype(BF16)
+    dgu_out[:, FF:] = (hidden * gate * sig).astype(BF16)
+    written.append(pltpu.make_async_copy(dgu_out, dgu_hbm.at[0, 0], loc.at[3]))
+    written[-1].start()
 
     for k in range(1, NP):
         other, _ = column(k)
         send(fs.at[other], fr.at[other], f_ss.at[k], f_rs.at[other], partner).wait_recv()
     for n in range(4):
         dkv_out[:, n, :] = fr[2 * n] + fr[2 * n + 1]
+    written.append(pltpu.make_async_copy(dkv_out, dkv_hbm, loc.at[4]))
+    written[-1].start()
 
     for copy in sends:
         copy.wait_send()
+    for n, cut in enumerate(cuts):
+        for k in order:
+            mine = tb.at[y, :, cut]
+            send(mine, mine, t_ss.at[n, k], t_rs.at[n, y], partner).wait_send()
+            send(
+                outgoing.at[n, own], incoming.at[n, own], a_ss.at[n, k], a_rs.at[n, d], partner
+            ).wait_send()
+    for copy in written:
+        copy.wait()
 
     @pl.loop(0, NZ)
     def _(j):
@@ -362,8 +384,11 @@
         kernel,
         out_shape=shapes,
         in_specs=[pl.BlockSpec(memory_space=pl.ANY)] * 8,
-        out_specs=tuple([pl.BlockSpec(memory_space=vmem)] * 3),
+        out_specs=tuple([pl.BlockSpec(memory_space=pl.ANY)] * 3),
         scratch_shapes=[
+            vmem((ROWS, HEAD), BF16),
+            vmem((2, 4, 2 * HEAD), F32),
+            vmem((SLOTS, 2 * FF), BF16),
             vmem((2, ROWS, HEAD), BF16),
             vmem((NZ, 2, SUB, HEAD), BF16),
             vmem((2, NP, ROWS, HEAD), BF16),
@@ -384,6 +409,7 @@
             vmem((SLOTS, 2 * FF), BF16),
             vmem((FF, WIDTH), BF16),
             vmem((NP, 16, SIDE + EXTRA), BF16),
+            vmem((2, 2, SLOTS, SLOTS), BF16),
             vmem((2, SLOTS, SIDE), BF16),
             vmem((2, SLOTS, SIDE), BF16),
             dma((8,)),

time: 56.3 us -> 53.8 us (0.956)
  the two profiles are of different devices: /device:TPU:64 before, /device:TPU:1 now
where the time goes in v3:
time: 53.8 us; the launch traced here: 53.5 us
  Pallas kernels  52.9 us (98%)
  between operations  0.64 us (1%)
    pallas_call x1, Pallas kernels, body(): pl.pallas_call(kernel, out_shape=shapes, in_specs=[pl.BlockSpec(memory_sp...  51 us
    pallas_call x1, Pallas kernels, body(): pl.pallas_call(store_kernel, out_shape=shapes, in_specs=[pl.BlockSpec(mem...  1.81 us

profile of v3, /device:TPU:1, one launch (start us, length us, event | category | flops | bytes accessed | tf_op | source)
XLA Modules:
  0.0 53.5 jit_solution(11849727462984143947)
XLA Ops:
  0.6 51.0 %layer_backward.1 = (bf16[128,128]{1,0:T(8,128)(2,1)}, f32[2,4,256]{2,1,0:T(4,128)}, bf16[1,1,128,1536]{3,2,1,0:T(8,128)(2,1)}) custom-call(bf16[128,128]{1,0:T(8,128)(2,1)} %q_ref.1, bf16[2,128,512]{2,1,0:T(8,128)(2,1)} %kv_ref.1, bf16[128,128]{1,0:T(8,128)(2,1)} %do_ref.1, bf16[8,4096]{1,0:T(8,128)(2,1)} %tok_ref.1, s32[8,8]{1,0:T(8,128)} %ids_ref.1, ...), custom_call_target="tpu_custom_call" | custom-call | tf_op jit(solution)/shard_map/layer_backward/pallas_call | solution.py:383
  51.7 1.8 %store.1 = (bf16[128,128]{1,0:T(8,128)(2,1)}, f32[2,4,256]{2,1,0:T(4,128)}, bf16[1,1,128,1536]{3,2,1,0:T(8,128)(2,1)}) custom-call(bf16[128,128]{1,0:T(8,128)(2,1)} %get-tuple-element.6.a_ref, f32[2,4,256]{2,1,0:T(4,128)} %get-tuple-element.7.b_ref, bf16[1,1,128,1536]{3,2,1,0:T(8,128)(2,1)} %get-tuple-element.8.c_ref), custom_call_target="tpu_custom_call" | custom-call | tf_op jit(solution)/shard_map/store/pallas_call | solution.py:426

commit v4 on v3

--- a/solution.py
+++ b/solution.py
@@ -137,9 +137,10 @@
         copy.start()
         sends.append(copy)
 
-    for k in order:
+    for k in (4, 2, 6):
         _, device = row(k)
         start(send(qd.at[:, d], qd.at[:, d], x_ss.at[k], x_rs.at[d], device))
+    start(send(qd.at[:, d], qd.at[:, d], x_ss.at[1], x_rs.at[d], partner))
     def send_tokens():
         for n, cut in enumerate(cuts):
             for k in order:
@@ -150,9 +151,16 @@
     late = z >= LATE
     pl.when(jnp.logical_not(late))(send_tokens)
 
-    for k in range(1, NP):
+    for k in (2, 6, 4):
         other, _ = row(k)
-        send(qd.at[:, other], qd.at[:, other], x_ss.at[k], x_rs.at[other], partner).wait_recv()
+        theirs = qd.at[:, other]
+        send(theirs, theirs, x_ss.at[k], x_rs.at[other], partner).wait_recv()
+        start(send(theirs, theirs, x_ss.at[k - 1 if k > 2 else 7], x_rs.at[other], partner))
+    twin = d + 1 - 2 * lax.rem(d, 2)
+    for k in range(0, NP, 2):
+        other = lax.rem(twin + k, NP)
+        theirs = qd.at[:, other]
+        send(theirs, theirs, x_ss.at[0], x_rs.at[other], partner).wait_recv()
 
     @pl.loop(0, NZ)
     def _(j):
@@ -232,6 +240,8 @@
         other, _ = row(k)
         send(stats.at[other], stats.at[other], st_ss.at[k], st_rs.at[other], partner).wait_recv()
 
+    pl.when(late)(send_tokens)
+
     top = stats[0, 0:NP]
     for n in range(1, NP):
         top = jnp.maximum(top, stats[n, 0:NP])
@@ -253,8 +263,6 @@
         @pl.when(j < z)
         def _():
             send(zs.at[j], zr.at[z], z_ss.at[j], z_rs.at[z], {"ctx": j, "exp": e}).start()
-
-    pl.when(late)(send_tokens)
 
     keys_t = keys.astype(F32).T.astype(BF16)
     for h in range(NP):
@@ -306,9 +314,11 @@
     for n in range(NP):
         fs[n] = summed[2 * n : 2 * n + 2]
     fr[y] = fs[y]
+    last = []
     for k in range(1, NP):
         other, device = column(k)
-        start(send(fs.at[other], fr.at[y], f_ss.at[k], f_rs.at[y], device))
+        last.append(send(fs.at[other], fr.at[y], f_ss.at[k], f_rs.at[y], device))
+        last[-1].start()
 
     dq = dqs[d].astype(F32)
     for k in range(1, NP):
@@ -326,14 +336,6 @@
     dgu_out[:, :FF] = (hidden * up * sig * (1.0 + gate * (1.0 - sig))).astype(BF16)
     dgu_out[:, FF:] = (hidden * gate * sig).astype(BF16)
     written.append(pltpu.make_async_copy(dgu_out, dgu_hbm.at[0, 0], loc.at[3]))
-    written[-1].start()
-
-    for k in range(1, NP):
-        other, _ = column(k)
-        send(fs.at[other], fr.at[other], f_ss.at[k], f_rs.at[other], partner).wait_recv()
-    for n in range(4):
-        dkv_out[:, n, :] = fr[2 * n] + fr[2 * n + 1]
-    written.append(pltpu.make_async_copy(dkv_out, dkv_hbm, loc.at[4]))
     written[-1].start()
 
     for copy in sends:
@@ -345,8 +347,6 @@
             send(
                 outgoing.at[n, own], incoming.at[n, own], a_ss.at[n, k], a_rs.at[n, d], partner
             ).wait_send()
-    for copy in written:
-        copy.wait()
 
     @pl.loop(0, NZ)
     def _(j):
@@ -358,15 +358,31 @@
         def _():
             send(zs.at[j], zr.at[j], z_ss.at[j], z_rs.at[j], partner).wait_send()
 
-
-def store_kernel(a_ref, b_ref, c_ref, a_out, b_out, c_out, sems):
-    copies = [
-        pltpu.make_async_copy(src, dst, sems.at[n])
-        for n, (src, dst) in enumerate(((c_ref, c_out), (a_ref, a_out), (b_ref, b_out)))
-    ]
-    for copy in copies:
+    for k in range(1, NP):
+        other, _ = column(k)
+        send(fs.at[other], fr.at[other], f_ss.at[k], f_rs.at[other], partner).wait_recv()
+    for n in range(4):
+        dkv_out[:, n, :] = fr[2 * n] + fr[2 * n + 1]
+    written.append(pltpu.make_async_copy(dkv_out, dkv_hbm, loc.at[4]))
+    written[-1].start()
+    for copy in last:
+        copy.wait_send()
+    for copy in written:
+        copy.wait()
+
+
+def store_kernel(a_ref, b_ref, c_ref, a_out, b_out, c_out, a_v, b_v, c_v, sems):
+    half = [pl.ds(n * SLOTS // 2, SLOTS // 2) for n in range(2)]
+    steps = [(c_ref.at[0, 0, h], c_v.at[h], c_out.at[0, 0, h]) for h in half]
+    steps += [(a_ref, a_v, a_out), (b_ref, b_v, b_out)]
+    loads = [pltpu.make_async_copy(s[0], s[1], sems.at[n]) for n, s in enumerate(steps)]
+    stores = [pltpu.make_async_copy(s[1], s[2], sems.at[4 + n]) for n, s in enumerate(steps)]
+    for copy in loads:
         copy.start()
-    for copy in copies:
+    for load, store in zip(loads, stores):
+        load.wait()
+        store.start()
+    for copy in stores:
         copy.wait()
 
 
@@ -426,9 +442,15 @@
     return pl.pallas_call(
         store_kernel,
         out_shape=shapes,
-        in_specs=[pl.BlockSpec(memory_space=vmem)] * 3,
+        in_specs=[pl.BlockSpec(memory_space=pl.ANY)] * 3,
         out_specs=tuple([pl.BlockSpec(memory_space=pl.ANY)] * 3),
-        scratch_shapes=[dma((3,))],
+        scratch_shapes=[
+            vmem((ROWS, HEAD), BF16),
+            vmem((2, 4, 2 * HEAD), F32),
+            vmem((SLOTS, 2 * FF), BF16),
+            dma((8,)),
+        ],
+        compiler_params=pltpu.CompilerParams(vmem_limit_bytes=60 * 1024 * 1024),
         name="store",
     )(*outs)
 

time: 53.8 us -> 53.4 us (level)
  no operation moved by 1% of the time
where the time goes in v4:
time: 53.4 us; the launch traced here: 53.2 us
  Pallas kernels  52.6 us (99%)
  between operations  0.64 us (1%)
    pallas_call x1, Pallas kernels, body(): pl.pallas_call(kernel, out_shape=shapes, in_specs=[pl.BlockSpec(memory_sp...  50.8 us
    pallas_call x1, Pallas kernels, body(): pl.pallas_call(store_kernel, out_shape=shapes, in_specs=[pl.BlockSpec(mem...  1.77 us

profile of v4, /device:TPU:1, one launch (start us, length us, event | category | flops | bytes accessed | tf_op | source)
XLA Modules:
  0.0 53.2 jit_solution(1522353170931323320)
XLA Ops:
  0.6 50.8 %layer_backward.1 = (bf16[128,128]{1,0:T(8,128)(2,1)}, f32[2,4,256]{2,1,0:T(4,128)}, bf16[1,1,128,1536]{3,2,1,0:T(8,128)(2,1)}) custom-call(bf16[128,128]{1,0:T(8,128)(2,1)} %q_ref.1, bf16[2,128,512]{2,1,0:T(8,128)(2,1)} %kv_ref.1, bf16[128,128]{1,0:T(8,128)(2,1)} %do_ref.1, bf16[8,4096]{1,0:T(8,128)(2,1)} %tok_ref.1, s32[8,8]{1,0:T(8,128)} %ids_ref.1, ...), custom_call_target="tpu_custom_call" | custom-call | tf_op jit(solution)/shard_map/layer_backward/pallas_call | solution.py:399
  51.5 1.8 %store.1 = (bf16[128,128]{1,0:T(8,128)(2,1)}, f32[2,4,256]{2,1,0:T(4,128)}, bf16[1,1,128,1536]{3,2,1,0:T(8,128)(2,1)}) custom-call(bf16[128,128]{1,0:T(8,128)(2,1)} %get-tuple-element.6.a_ref, f32[2,4,256]{2,1,0:T(4,128)} %get-tuple-element.7.b_ref, bf16[1,1,128,1536]{3,2,1,0:T(8,128)(2,1)} %get-tuple-element.8.c_ref), custom_call_target="tpu_custom_call" | custom-call | tf_op jit(solution)/shard_map/store/pallas_call | solution.py:442

commit v5 on v4

--- a/solution.py
+++ b/solution.py
@@ -300,7 +300,6 @@
             )
         return total
 
-    hidden = down_part(0)
 
     @pl.loop(0, NZ)
     def _(j):
@@ -329,7 +328,7 @@
     written = [pltpu.make_async_copy(dq_out, dq_hbm, loc.at[2])]
     written[-1].start()
 
-    hidden += down_part(1)
+    hidden = down_part(0) + down_part(1)
     gate = saved_v[:, :FF].astype(F32)
     up = saved_v[:, FF:].astype(F32)
     sig = 1.0 / (1.0 + jnp.exp(-gate))

time: 53.4 us -> 53.4 us (level)
  no operation moved by 1% of the time
where the time goes in v5:
time: 53.4 us; the launch traced here: 53.2 us
  Pallas kernels  52.6 us (99%)
  between operations  0.64 us (1%)
    pallas_call x1, Pallas kernels, body(): pl.pallas_call(kernel, out_shape=shapes, in_specs=[pl.BlockSpec(memory_sp...  50.8 us
    pallas_call x1, Pallas kernels, body(): pl.pallas_call(store_kernel, out_shape=shapes, in_specs=[pl.BlockSpec(mem...  1.77 us

profile of v5, /device:TPU:1, one launch (start us, length us, event | category | flops | bytes accessed | tf_op | source)
XLA Modules:
  0.0 53.2 jit_solution(10286774666032668640)
XLA Ops:
  0.6 50.8 %layer_backward.1 = (bf16[128,128]{1,0:T(8,128)(2,1)}, f32[2,4,256]{2,1,0:T(4,128)}, bf16[1,1,128,1536]{3,2,1,0:T(8,128)(2,1)}) custom-call(bf16[128,128]{1,0:T(8,128)(2,1)} %q_ref.1, bf16[2,128,512]{2,1,0:T(8,128)(2,1)} %kv_ref.1, bf16[128,128]{1,0:T(8,128)(2,1)} %do_ref.1, bf16[8,4096]{1,0:T(8,128)(2,1)} %tok_ref.1, s32[8,8]{1,0:T(8,128)} %ids_ref.1, ...), custom_call_target="tpu_custom_call" | custom-call | tf_op jit(solution)/shard_map/layer_backward/pallas_call | solution.py:398
  51.5 1.8 %store.1 = (bf16[128,128]{1,0:T(8,128)(2,1)}, f32[2,4,256]{2,1,0:T(4,128)}, bf16[1,1,128,1536]{3,2,1,0:T(8,128)(2,1)}) custom-call(bf16[128,128]{1,0:T(8,128)(2,1)} %get-tuple-element.6.a_ref, f32[2,4,256]{2,1,0:T(4,128)} %get-tuple-element.7.b_ref, bf16[1,1,128,1536]{3,2,1,0:T(8,128)(2,1)} %get-tuple-element.8.c_ref), custom_call_target="tpu_custom_call" | custom-call | tf_op jit(solution)/shard_map/store/pallas_call | solution.py:441
